TPU v7x, 256 devices: a whole 4x4x8 slice. The times are simulated.
256 devices in a mesh: dp: 16 (over y_lo, z), factor: 16 (over x, y_hi, core).
Axes of the slice: x: 4, y: 4 (y_hi: 2, y_lo: 2; y = y_hi * 2 + y_lo), z: 8, core: 2. Of those that a mesh axis runs over, the one named last changes fastest.
Arguments:
- train_inputs: bfloat16 [128, 8, 64, 320], P('dp'), may hold values from -6 to 6
- train_cotangents: bfloat16 [128, 8, 64, 320], P('dp'), may hold values from -0.26367188 to 0.26367188
- query_inputs: bfloat16 [16, 8, 64, 320], P('dp'), may hold values from -6 to 6
- query_cotangents: bfloat16 [16, 8, 64, 320], P('dp'), may hold values from -0.26367188 to 0.26367188
- timesteps: int32 [128], P('dp'), may hold values from 0 to 999
- input_basis: bfloat16 [2880, 2880], P('dp', 'factor'), may hold values from -0.109375 to 0.109375
- output_basis: bfloat16 [320, 320], replicated, may hold values from -0.3125 to 0.3125
- eigenvalues: float32 [320, 2880], P(None, 'factor'), may hold values from 0.1 to 10
Outputs:
- scores: float32 [128], P('dp')
- query_proj: float32 [320, 2880], P(None, 'factor')
All inputs are finite; a program needn't handle non-finite values.
Results may differ from a plain program's by a relative error of at most 0.0037.
Values may be sent and summed in bfloat16 or wider, within the bound.
A program may use at most 192 MiB of HBM per device.

v0:
```python
import math
import jax
import jax.numpy as jnp
from jax import lax
from jax.sharding import PartitionSpec as P

damping = 0.01


def patch_matrix(activations):
    batch, rows_count, cols_count, channels = activations.shape
    padded = jnp.pad(activations, ((0, 0), (1, 1), (1, 1), (0, 0)))
    taps = [
        padded[:, row_off : row_off + rows_count, col_off : col_off + cols_count, :]
        for row_off in range(3)
        for col_off in range(3)
    ]
    return jnp.concatenate(taps, axis=-1).reshape(batch * rows_count * cols_count, 9 * channels)


def on_device(
    train_inputs,
    train_cotangents,
    query_inputs,
    query_cotangents,
    timesteps,
    input_basis,
    output_basis,
    eigenvalues,
):
    high = lax.Precision.HIGHEST
    channels = output_basis.shape[0]
    width = input_basis.shape[0] * lax.axis_size("dp")
    batch = train_inputs.shape[0]
    positions = train_inputs.shape[1] * train_inputs.shape[2]
    panel_width = input_basis.shape[1]
    train_patches = patch_matrix(train_inputs)
    query_patches = patch_matrix(query_inputs)
    query_flat = query_cotangents.reshape(-1, channels)
    partial_query = jnp.dot(query_flat.T, query_patches, preferred_element_type=jnp.float32)
    count = query_inputs.shape[0] * lax.axis_size("dp")
    query_grad = lax.psum(partial_query, "dp") / count
    piece = lax.all_gather(input_basis, "dp", axis=0, tiled=True)
    query_part = jnp.dot(query_grad, piece.astype(jnp.float32), precision=high)
    projected = jnp.dot(train_patches, piece, preferred_element_type=jnp.float32)
    basis_out = output_basis.astype(jnp.float32)
    query_proj = jnp.dot(basis_out.T, query_part, precision=high) / (eigenvalues + damping)
    rotated = jnp.dot(
        train_cotangents.reshape(-1, channels), output_basis, preferred_element_type=jnp.float32
    )
    rotated = rotated.astype(jnp.bfloat16).reshape(batch, positions, channels)
    projected = projected.astype(jnp.bfloat16).reshape(batch, positions, panel_width)
    train_proj = jnp.einsum("bpc,bpk->bck", rotated, projected, preferred_element_type=jnp.float32)
    partial_scores = jnp.einsum("bck,ck->b", train_proj, query_proj, precision=high)
    raw_scores = lax.psum(partial_scores, "factor")
    phase = (timesteps.astype(jnp.float32) / 1000.0 + 0.008) / 1.008 * (math.pi / 2)
    weight = jnp.sin(phase)
    scores = raw_scores * weight / math.sqrt(channels * width)
    return (scores, query_proj)


def solution(mesh):
    in_specs = (
        P("dp", None, None, None),
        P("dp", None, None, None),
        P("dp", None, None, None),
        P("dp", None, None, None),
        P("dp"),
        P("dp", "factor"),
        P(),
        P(None, "factor"),
    )
    out_specs = (P("dp"), P(None, "factor"))
    return jax.shard_map(
        on_device, mesh=mesh, in_specs=in_specs, out_specs=out_specs, check_vma=False
    )
```

profile of v0, /device:TPU:1, one launch (start us, length us, event | category | flops | bytes accessed | tf_op | source)
XLA Modules:
  0.0 234.6 jit_solution(13893424670948783343)
XLA Ops:
  7.2 0.0 copy-start
  7.2 0.0 all-reduce.4.cloned.1.call-start
  7.2 4.6 %pad_slice_fusion.8 = (bf16[1,8,64,320]{3,2,1,0:T(8,128)(2,1)}, bf16[1,8,64,320]{3,2,1,0:T(8,128)(2,1)}, bf16[1,8,64,320]{3,2,1,0:T(8,128)(2,1)}, bf16[1,8,64,32...) fusion(bf16[1,8,64,320]{3,2,1,0:T(8,128)(2,1)} %param.10), kind=kLoop, calls=%fused_computation.25 | loop fusion | bytes 2949120 | tf_op jit(solution)/shard_map/slice | solution.py:14
  11.9 6.2 %concatenate.7 = bf16[1,8,64,2880]{3,2,1,0:T(8,128)(2,1)} concatenate(bf16[1,8,64,320]{3,2,1,0:T(8,128)(2,1)} %get-tuple-element.17, bf16[1,8,64,320]{3,2,1,0:T(8,128)(2,1)} %get-tuple-element.11, bf16[1,8,64,320]{3,2,1,0:T(8,128)(2,1)} %get-tuple-element.12, bf16[1,8,64,320]{3,2,1,0:T(8,128)(2,1)} %get-tuple-element.13, bf16[1,8,64,320]{3,2,1,0:T(8,128)(2,1)S(1)} %copy-done.2, ...), dimensions={3} | concatenate | bytes 5898240 | tf_op jit(solution)/shard_map/concatenate | solution.py:18
  18.0 5.1 %convolution_bitcast_fusion = f32[320,2880]{1,0:T(8,128)} fusion(bf16[1,8,64,2880]{3,2,1,0:T(8,128)(2,1)} %concatenate.7, bf16[1,8,64,320]{3,2,1,0:T(8,128)(2,1)} %param.11), kind=kOutput, calls=%fused_computation.10 | convolution fusion | flops 943718400 | bytes 6963200 | tf_op jit(solution)/shard_map/dot_general | solution.py:40
  23.1 0.0 all-reduce.4.cloned.1.call-update
  23.1 0.9 copy-done.6
  24.0 52.8 %all-gather = bf16[16,180,180]{2,1,0:T(8,128)(2,1)} all-gather(bf16[1,180,180]{2,1,0:T(8,128)(2,1)S(1)} %bitcast.43), channel_id=1, replica_groups=mesh['dp'=16,'factor'=16] {'dp'}, dimensions={0}, use_global_device_ids=true | all-gather | bytes 1101600 | tf_op jit(solution)/shard_map/all_gather | solution.py:43
  76.8 3.5 %reshape.35 = bf16[2880,180]{1,0:T(8,128)(2,1)} reshape(bf16[16,180,180]{2,1,0:T(8,128)(2,1)} %all-gather) | data formatting | bytes 2073600
  80.3 20.4 %pad_slice_fusion = (bf16[8,8,64,320]{3,2,1,0:T(8,128)(2,1)}, bf16[8,8,64,320]{3,2,1,0:T(8,128)(2,1)}, bf16[8,8,64,320]{3,2,1,0:T(8,128)(2,1)}, bf16[8,8,64,320]...) fusion(bf16[8,8,64,320]{3,2,1,0:T(8,128)(2,1)} %param.8), kind=kLoop, calls=%fused_computation.1 | loop fusion | bytes 23592960 | tf_op jit(solution)/shard_map/slice | solution.py:14
  100.7 37.5 %concatenate.6 = bf16[8,8,64,2880]{3,2,1,0:T(8,128)(2,1)} concatenate(bf16[8,8,64,320]{3,2,1,0:T(8,128)(2,1)} %get-tuple-element.9, bf16[8,8,64,320]{3,2,1,0:T(8,128)(2,1)} %get-tuple-element.3, bf16[8,8,64,320]{3,2,1,0:T(8,128)(2,1)} %get-tuple-element.4, bf16[8,8,64,320]{3,2,1,0:T(8,128)(2,1)} %get-tuple-element.5, bf16[8,8,64,320]{3,2,1,0:T(8,128)(2,1)} %param.8, ...), dimensions={3} | concatenate | bytes 47185920 | tf_op jit(solution)/shard_map/concatenate | solution.py:18
  138.2 14.1 %convolution_convert_fusion.1 = bf16[4096,180]{0,1:T(8,128)(2,1)} fusion(bf16[4096,2880]{1,0:T(8,128)(2,1)} %bitcast.38, bf16[2880,180]{1,0:T(8,128)(2,1)} %reshape.35), kind=kOutput, calls=%fused_computation.9 | convolution fusion | flops 4247470080 | bytes 26104320 | tf_op jit(solution)/shard_map/dot_general | solution.py:45
  152.3 2.1 copy.18
  154.3 0.1 slice_bitcast_fusion
  154.5 1.6 convolution_convert_fusion
  156.0 2.7 %fusion.3 = f32[8,320,180]{1,2,0:T(8,128)} fusion(bf16[40,8,8,512]{3,2,1,0:T(8,128)(2,1)S(1)} %bitcast.39, bf16[8,512,180]{1,0,2:T(8,128)(2,1)S(1)} %slice_bitcast_fusion), kind=kOutput, calls=%fused_computation.14 | convolution fusion | flops 471859200 | bytes 5939200 | tf_op jit(solution)/shard_map/bpc,bpk->bck/dot_general | solution.py:53
  158.8 15.3 %all-reduce.4.cloned.1.call-done = f32[320,2880]{1,0:T(8,128)} async-done(((f32[320,2880]{1,0:T(8,128)}), f32[320,2880]{1,0:T(8,128)}) %all-reduce.4.cloned.1.call-update) | async-done | bytes 3686416 | tf_op jit(solution)/shard_map/psum | solution.py:42
  174.1 5.4 %fusion = f32[320,180]{0,1:T(8,128)S(1)} fusion(bf16[2880,180]{1,0:T(8,128)(2,1)} %reshape.35, f32[320,2880]{1,0:T(8,128)} %all-reduce.4.cloned.1.call-done), kind=kOutput, calls=%fused_computation.11 | convolution fusion | flops 1991577600 | bytes 4953600 | tf_op jit(solution)/shard_map/dot_general | solution.py:44
  179.4 0.0 copy-start.8
  179.5 0.5 fusion.10
  179.9 0.0 copy-start.3
  180.0 4.9 %fusion.11 = f32[8]{0:T(128)S(1)} fusion(f32[8,320,180]{1,2,0:T(8,128)S(1)} %copy-done.1, f32[320,180,1]{0,1,2:T(8,128)S(1)} %bitcast.42), kind=kOutput, calls=%fused_computation.24 | convolution fusion | flops 5529600 | bytes 2073632 | tf_op jit(solution)/shard_map/bck,ck->b/dot_general | solution.py:54
  184.8 42.3 %psum.15 = f32[8]{0:T(128)S(1)} all-reduce(f32[8]{0:T(128)S(1)} %fusion.11), channel_id=1, replica_groups=mesh['dp'=16,'factor'=16] {'factor'}, use_global_device_ids=true, to_apply=%region_1.2 | all-reduce | flops 8 | bytes 64 | tf_op jit(solution)/shard_map/psum | solution.py:55
  227.2 0.6 multiply_multiply_fusion
  (14 shorter events, 0.0 us)
Async XLA Ops:
  7.2 147.3 %copy-start = (bf16[8,8,64,320]{3,2,1,0:T(8,128)(2,1)S(1)}, bf16[8,8,64,320]{3,2,1,0:T(8,128)(2,1)}, u32[]{:S(2)}) copy-start(bf16[8,8,64,320]{3,2,1,0:T(8,128)(2,1)} %param.9) | copy-start | bytes 7864324
  7.2 4.7 %copy-start.2 = (bf16[1,8,64,320]{3,2,1,0:T(8,128)(2,1)S(1)}, bf16[1,8,64,320]{3,2,1,0:T(8,128)(2,1)}, u32[]{:S(2)}) copy-start(bf16[1,8,64,320]{3,2,1,0:T(8,128)(2,1)} %param.10) | copy-start | bytes 983044
  7.2 166.9 %all-reduce.4.cloned.1.call-start = ((), (), s32[]{:S(2)}) async-start(), calls=%async_computation | async-start | bytes 7536640 | tf_op jit(solution)/shard_map/psum | solution.py:42
  23.1 0.9 copy-start.6
  152.3 2.2 copy-start.4
  174.1 5.4 %copy-start.5 = (bf16[320,320]{1,0:T(8,128)(2,1)S(1)}, bf16[320,320]{1,0:T(8,128)(2,1)}, u32[]{:S(2)}) copy-start(bf16[320,320]{1,0:T(8,128)(2,1)} %param.14) | copy-start | bytes 614404
  174.1 5.4 %copy-start.7 = (f32[320,180]{0,1:T(8,128)S(1)}, f32[320,180]{0,1:T(8,128)}, u32[]{:S(2)}) copy-start(f32[320,180]{0,1:T(8,128)} %param.15) | copy-start | bytes 691204
  174.1 5.9 %copy-start.1 = (f32[8,320,180]{1,2,0:T(8,128)S(1)}, f32[8,320,180]{1,2,0:T(8,128)}, u32[]{:S(2)}) copy-start(f32[8,320,180]{1,2,0:T(8,128)} %fusion.3) | copy-start | bytes 5529604
  179.4 47.7 %copy-start.8 = (s32[8]{0:T(128)S(1)}, s32[8]{0:T(128)}, u32[]{:S(2)}) copy-start(s32[8]{0:T(128)} %param.12) | copy-start | bytes 100
  179.9 47.8 %copy-start.3 = (f32[320,180]{0,1:T(8,128)}, f32[320,180]{0,1:T(8,128)S(1)}, u32[]{:S(2)}) copy-start(f32[320,180]{0,1:T(8,128)S(1)} %fusion.10) | copy-start | bytes 691204
Sparse Core Ops, SparseCore 0:
  23.2 150.7 all-reduce.3
where the time goes:
time: 238 us; the launch traced here: 235 us
  blocking collectives  95.1 us (40%)
  local copies, waits for them, and re-layouts  75.3 us (32%)
  matrix products  34.2 us (14%)
  waiting for transfers between devices  15.3 us (6%)
  between operations  14.1 us (6%)
    all_gather x1, blocking collectives, on_device(): piece = lax.all_gather(input_basis, 'dp', axis=0, tiled=True)  52.8 us
    concatenate x2, local copies, waits for them, and re-layouts, patch_matrix(): jnp.concatenate(taps, axis=-1)  43.6 us
    psum x1, blocking collectives, on_device(): raw_scores = lax.psum(partial_scores, 'factor')  42.3 us
    slice x2, local copies, waits for them, and re-layouts, patch_matrix(): padded[:, row_off:row_off + rows_count, col_off:col_off + cols_count, :]  25.1 us
    psum x1, waiting for transfers between devices, on_device(): query_grad = lax.psum(partial_query, 'dp') / count  15.3 us
    dot_general x1, matrix products, on_device(): jnp.dot(train_patches, piece, preferred_element_type=jnp.float32)  14.1 us
    unnamed x20, local copies, waits for them, and re-layouts  6.49 us
    dot_general x1, matrix products, on_device(): query_part = jnp.dot(query_grad, piece.astype(jnp.float32), precision=high)  5.35 us
  transfers between devices with their start and end apart: 1, of which 1 were waited for; matrix products, arithmetic and copies ran while one was open for 35% of the time, Pallas kernels for 0%

commit v1 on v0

--- a/solution.py
+++ b/solution.py
@@ -40,7 +40,9 @@
     partial_query = jnp.dot(query_flat.T, query_patches, preferred_element_type=jnp.float32)
     count = query_inputs.shape[0] * lax.axis_size("dp")
     query_grad = lax.psum(partial_query, "dp") / count
-    piece = lax.all_gather(input_basis, "dp", axis=0, tiled=True)
+    piece = jnp.concatenate(
+        lax.all_to_all(jnp.stack([input_basis] * lax.axis_size("dp")), "dp", 0, 0), axis=0
+    )
     query_part = jnp.dot(query_grad, piece.astype(jnp.float32), precision=high)
     projected = jnp.dot(train_patches, piece, preferred_element_type=jnp.float32)
     basis_out = output_basis.astype(jnp.float32)

time: 238 us -> 248 us (1.042)
  blocking collectives: 95.1 us -> 42.3 us
  waiting for transfers between devices: 15.3 us -> 60.3 us
  starting transfers between devices: 0.04 us -> 10.2 us
  local copies, waits for them, and re-layouts: 75.3 us -> 79 us
  matrix products: 34.2 us -> 37.7 us
    all_gather x1 -> x0, blocking collectives: 52.8 us -> none  [on_device(): piece = lax.all_gather(input_basis, 'dp', axis=0, tiled=True)]
    psum x1, waiting for transfers between devices: 15.3 us -> 60.3 us  [on_device(): query_grad = lax.psum(partial_query, 'dp') / count]
    all_to_all x0 -> x1, starting transfers between devices: none -> 10.2 us  [on_device(): lax.all_to_all(jnp.stack([input_basis] * lax.axis_size('dp')), 'dp', 0, 0)]
    reshape x0 -> x1, local copies, waits for them, and re-layouts: none -> 4.02 us  [on_device(): jnp.concatenate(lax.all_to_all(jnp.stack([input_basis] * lax.axis_size('d...]
    unnamed x20, local copies, waits for them, and re-layouts: 6.49 us -> 3.46 us
    all_to_all x0 -> x1, local copies, waits for them, and re-layouts: none -> 2.82 us  [on_device(): lax.all_to_all(jnp.stack([input_basis] * lax.axis_size('dp')), 'dp', 0, 0)]
  transfers between devices with their start and end apart: 1 -> 2, of which waited for: 1 -> 1; matrix products, arithmetic and copies ran while one was open for 35% -> 42% of each run, Pallas kernels for 0% -> 0%
where the time goes in v1:
time: 248 us; the launch traced here: 244 us
  local copies, waits for them, and re-layouts  79 us (32%)
  waiting for transfers between devices  60.3 us (24%)
  blocking collectives  42.3 us (17%)
  matrix products  37.7 us (15%)
  between operations  14.2 us (6%)
  starting transfers between devices  10.2 us (4%)
    psum x1, waiting for transfers between devices, on_device(): query_grad = lax.psum(partial_query, 'dp') / count  60.3 us
    concatenate x2, local copies, waits for them, and re-layouts, patch_matrix(): jnp.concatenate(taps, axis=-1)  43.7 us
    psum x1, blocking collectives, on_device(): raw_scores = lax.psum(partial_scores, 'factor')  42.3 us
    slice x2, local copies, waits for them, and re-layouts, patch_matrix(): padded[:, row_off:row_off + rows_count, col_off:col_off + cols_count, :]  22.8 us
    dot_general x1, matrix products, on_device(): jnp.dot(train_patches, piece, preferred_element_type=jnp.float32)  16.6 us
    all_to_all x1, starting transfers between devices, on_device(): lax.all_to_all(jnp.stack([input_basis] * lax.axis_size('dp')), 'dp', 0, 0)  10.2 us
    dot_general x1, matrix products, on_device(): jnp.dot(query_flat.T, query_patches, preferred_element_type=jnp.float32)  5.06 us
    dot_general x1, matrix products, on_device(): query_part = jnp.dot(query_grad, piece.astype(jnp.float32), precision=high)  5.01 us
  transfers between devices with their start and end apart: 2, of which 1 were waited for; matrix products, arithmetic and copies ran while one was open for 42% of the time, Pallas kernels for 0%

profile of v1, /device:TPU:1, one launch (start us, length us, event | category | flops | bytes accessed | tf_op | source)
XLA Modules:
  0.0 244.4 jit_solution(14379280675896507618)
XLA Ops:
  7.2 1.8 copy.11
  9.0 2.1 stack.2
  11.1 10.2 %all-to-all-start = ((bf16[16,180,180]{1,2,0:T(8,128)(2,1)}), bf16[16,180,180]{1,2,0:T(8,128)(2,1)}, u32[]{:S(2)}, u32[]{:S(2)}) async-start(bf16[16,180,180]{1,2,0:T(8,128)(2,1)} %stack.2), calls=%async_computation | async-start | bytes 3014656 | tf_op jit(solution)/shard_map/all_to_all | solution.py:44
  21.3 0.0 all-reduce.4.cloned.1.call-start
  21.4 1.9 pad_slice_fusion.8
  23.3 6.2 %concatenate.7 = bf16[1,8,64,2880]{3,2,1,0:T(8,128)(2,1)} concatenate(bf16[1,8,64,320]{3,2,1,0:T(8,128)(2,1)} %get-tuple-element.17, bf16[1,8,64,320]{3,2,1,0:T(8,128)(2,1)} %get-tuple-element.11, bf16[1,8,64,320]{3,2,1,0:T(8,128)(2,1)} %get-tuple-element.12, bf16[1,8,64,320]{3,2,1,0:T(8,128)(2,1)} %get-tuple-element.13, bf16[1,8,64,320]{3,2,1,0:T(8,128)(2,1)S(1)} %copy-done.3, ...), dimensions={3} | concatenate | bytes 5898240 | tf_op jit(solution)/shard_map/concatenate | solution.py:18
  29.4 5.1 %convolution_bitcast_fusion = f32[320,2880]{1,0:T(8,128)} fusion(bf16[1,8,64,2880]{3,2,1,0:T(8,128)(2,1)} %concatenate.7, bf16[1,8,64,320]{3,2,1,0:T(8,128)(2,1)} %param.11), kind=kOutput, calls=%fused_computation.10 | convolution fusion | flops 943718400 | bytes 6963200 | tf_op jit(solution)/shard_map/dot_general | solution.py:40
  34.5 0.0 all-reduce.4.cloned.1.call-update
  34.5 20.9 %pad_slice_fusion = (bf16[8,8,64,320]{3,2,1,0:T(8,128)(2,1)}, bf16[8,8,64,320]{3,2,1,0:T(8,128)(2,1)}, bf16[8,8,64,320]{3,2,1,0:T(8,128)(2,1)}, bf16[8,8,64,320]...) fusion(bf16[8,8,64,320]{3,2,1,0:T(8,128)(2,1)} %param.8), kind=kLoop, calls=%fused_computation.1 | loop fusion | bytes 23592960 | tf_op jit(solution)/shard_map/slice | solution.py:14
  55.4 37.5 %concatenate.6 = bf16[8,8,64,2880]{3,2,1,0:T(8,128)(2,1)} concatenate(bf16[8,8,64,320]{3,2,1,0:T(8,128)(2,1)} %get-tuple-element.9, bf16[8,8,64,320]{3,2,1,0:T(8,128)(2,1)} %get-tuple-element.3, bf16[8,8,64,320]{3,2,1,0:T(8,128)(2,1)} %get-tuple-element.4, bf16[8,8,64,320]{3,2,1,0:T(8,128)(2,1)} %get-tuple-element.5, bf16[8,8,64,320]{3,2,1,0:T(8,128)(2,1)} %param.8, ...), dimensions={3} | concatenate | bytes 47185920 | tf_op jit(solution)/shard_map/concatenate | solution.py:18
  93.0 3.0 %convolution_convert_fusion = bf16[4096,320]{0,1:T(8,128)(2,1)} fusion(bf16[4096,320]{1,0:T(8,128)(2,1)S(1)} %bitcast.38, bf16[320,320]{1,0:T(8,128)(2,1)S(1)} %copy-done.5), kind=kOutput, calls=%fused_computation | convolution fusion | flops 840171520 | bytes 5447680 | tf_op jit(solution)/shard_map/dot_general | solution.py:50
  96.0 2.8 %copy.12 = bf16[16,180,180]{1,0,2:T(8,128)(2,1)} copy(bf16[16,180,180]{1,2,0:T(8,128)(2,1)} %all-to-all-done) | data formatting | bytes 2073600 | tf_op jit(solution)/shard_map/all_to_all | solution.py:44
  98.8 4.0 %reshape.32 = bf16[2880,180]{0,1:T(8,128)(2,1)} reshape(bf16[16,180,180]{1,0,2:T(8,128)(2,1)} %copy.12) | data formatting | bytes 2073600 | tf_op jit(solution)/shard_map/reshape | solution.py:43
  102.8 16.6 %convolution_convert_fusion.1 = bf16[4096,180]{0,1:T(8,128)(2,1)S(1)} fusion(bf16[4096,2880]{1,0:T(8,128)(2,1)} %bitcast.39, bf16[2880,180]{0,1:T(8,128)(2,1)} %reshape.32), kind=kOutput, calls=%fused_computation.9 | convolution fusion | flops 4247470080 | bytes 26104320 | tf_op jit(solution)/shard_map/dot_general | solution.py:47
  119.4 0.6 copy.18
  120.1 0.1 slice_bitcast_fusion
  120.2 1.0 copy-done.1
  121.2 2.7 %fusion.3 = f32[8,320,180]{1,2,0:T(8,128)} fusion(bf16[40,8,8,512]{3,2,1,0:T(8,128)(2,1)S(1)} %bitcast.40, bf16[8,512,180]{1,0,2:T(8,128)(2,1)S(1)} %slice_bitcast_fusion), kind=kOutput, calls=%fused_computation.14 | convolution fusion | flops 471859200 | bytes 5939200 | tf_op jit(solution)/shard_map/bpc,bpk->bck/dot_general | solution.py:55
  123.9 60.3 %all-reduce.4.cloned.1.call-done = f32[320,2880]{1,0:T(8,128)} async-done(((f32[320,2880]{1,0:T(8,128)}), f32[320,2880]{1,0:T(8,128)}) %all-reduce.4.cloned.1.call-update) | async-done | bytes 3686416 | tf_op jit(solution)/shard_map/psum | solution.py:42
  184.2 5.0 %fusion = f32[320,180]{0,1:T(8,128)S(1)} fusion(bf16[2880,180]{0,1:T(8,128)(2,1)} %reshape.32, f32[320,2880]{1,0:T(8,128)} %all-reduce.4.cloned.1.call-done), kind=kOutput, calls=%fused_computation.11 | convolution fusion | flops 1991577600 | bytes 4953600 | tf_op jit(solution)/shard_map/dot_general | solution.py:46
  189.2 0.5 fusion.10
  189.7 4.9 %fusion.11 = f32[8]{0:T(128)S(1)} fusion(f32[8,320,180]{1,2,0:T(8,128)S(1)} %copy-done.2, f32[320,180,1]{0,1,2:T(8,128)S(1)} %bitcast.43), kind=kOutput, calls=%fused_computation.24 | convolution fusion | flops 5529600 | bytes 2073632 | tf_op jit(solution)/shard_map/bck,ck->b/dot_general | solution.py:56
  194.6 42.3 %psum.15 = f32[8]{0:T(128)S(1)} all-reduce(f32[8]{0:T(128)S(1)} %fusion.11), channel_id=1, replica_groups=mesh['dp'=16,'factor'=16] {'factor'}, use_global_device_ids=true, to_apply=%region_1.2 | all-reduce | flops 8 | bytes 64 | tf_op jit(solution)/shard_map/psum | solution.py:57
  237.0 0.6 multiply_multiply_fusion
  (18 shorter events, 0.0 us)
Async XLA Ops:
  7.2 85.8 %copy-start = (bf16[8,8,64,320]{3,2,1,0:T(8,128)(2,1)S(1)}, bf16[8,8,64,320]{3,2,1,0:T(8,128)(2,1)}, u32[]{:S(2)}) copy-start(bf16[8,8,64,320]{3,2,1,0:T(8,128)(2,1)} %param.9) | copy-start | bytes 7864324
  7.2 14.2 %copy-start.3 = (bf16[1,8,64,320]{3,2,1,0:T(8,128)(2,1)S(1)}, bf16[1,8,64,320]{3,2,1,0:T(8,128)(2,1)}, u32[]{:S(2)}) copy-start(bf16[1,8,64,320]{3,2,1,0:T(8,128)(2,1)} %param.10) | copy-start | bytes 983044
  11.1 84.9 %all-to-all-start = ((bf16[16,180,180]{1,2,0:T(8,128)(2,1)}), bf16[16,180,180]{1,2,0:T(8,128)(2,1)}, u32[]{:S(2)}, u32[]{:S(2)}) async-start(bf16[16,180,180]{1,2,0:T(8,128)(2,1)} %stack.2), calls=%async_computation | async-start | bytes 3014656 | tf_op jit(solution)/shard_map/all_to_all | solution.py:44
  21.3 162.9 %all-reduce.4.cloned.1.call-start = ((), (), s32[]{:S(2)}) async-start(), calls=%async_computation.1 | async-start | bytes 7536640 | tf_op jit(solution)/shard_map/psum | solution.py:42
  55.4 37.5 %copy-start.5 = (bf16[320,320]{1,0:T(8,128)(2,1)S(1)}, bf16[320,320]{1,0:T(8,128)(2,1)}, u32[]{:S(2)}) copy-start(bf16[320,320]{1,0:T(8,128)(2,1)} %param.14) | copy-start | bytes 614404
  119.4 1.7 copy-start.1
  184.2 5.0 %copy-start.6 = (bf16[320,320]{1,0:T(8,128)(2,1)S(1)}, bf16[320,320]{1,0:T(8,128)(2,1)}, u32[]{:S(2)}) copy-start(bf16[320,320]{1,0:T(8,128)(2,1)} %param.14) | copy-start | bytes 614404
  184.2 5.0 %copy-start.7 = (f32[320,180]{0,1:T(8,128)S(1)}, f32[320,180]{0,1:T(8,128)}, u32[]{:S(2)}) copy-start(f32[320,180]{0,1:T(8,128)} %param.15) | copy-start | bytes 691204
  184.2 5.5 %copy-start.2 = (f32[8,320,180]{1,2,0:T(8,128)S(1)}, f32[8,320,180]{1,2,0:T(8,128)}, u32[]{:S(2)}) copy-start(f32[8,320,180]{1,2,0:T(8,128)} %fusion.3) | copy-start | bytes 5529604
  189.2 47.7 %copy-start.8 = (s32[8]{0:T(128)S(1)}, s32[8]{0:T(128)}, u32[]{:S(2)}) copy-start(s32[8]{0:T(128)} %param.12) | copy-start | bytes 100
  189.7 47.8 %copy-start.4 = (f32[320,180]{0,1:T(8,128)}, f32[320,180]{0,1:T(8,128)S(1)}, u32[]{:S(2)}) copy-start(f32[320,180]{0,1:T(8,128)S(1)} %fusion.10) | copy-start | bytes 691204
Sparse Core Ops, SparseCore 0:
  34.6 149.5 all-reduce.3
